TPU v7x, 32 devices: a whole 2x2x4 slice. The times are simulated.
32 devices in a mesh: ctx: 16 (over z, y, x), pipe: 2 (over core).
Axes of the slice: x: 2, y: 2, z: 4, core: 2. Of those that a mesh axis runs over, the one named last changes fastest.
Arguments:
- activations: float32 [2, 1, 2048, 4096], P('pipe', None, 'ctx'), may hold values from -6 to 6
- norm_gain: bfloat16 [2, 8, 4096], P('pipe', None, 'ctx'), may hold values from 0.5 to 2, as said below
- w_query: bfloat16 [2, 8, 4096, 512], P('pipe', None, 'ctx'), may hold values from -0.09375 to 0.09375
- w_keyval: bfloat16 [2, 8, 4096, 256], P('pipe', None, 'ctx'), may hold values from -0.09375 to 0.09375
- w_out: bfloat16 [2, 8, 512, 4096], P('pipe', None, None, 'ctx'), may hold values from -0.25 to 0.25
- segment_ids: int32 [1, 2048], replicated, may hold values from 0 to 3, as said below
- layer_order: int32 [2, 2], P(None, 'pipe'), may hold values from 0 to 7
Outputs:
- final_stream: float32 [2, 1, 2048, 4096], P('pipe', None, 'ctx')
Inputs may be any that keep to these rules, and one draw needn't show every extreme that they name: `segment_ids`: each row never falls; every document holds 1 to 1024 positions and the last one holds exactly 1024. `norm_gain`: positive.
All inputs are finite; a program needn't handle non-finite values.
Results may differ from a plain program's by a relative error of at most 0.015.
Values may be sent and summed in bfloat16 or wider, within the bound.
A program may use at most 128 MiB of HBM per device.

v0:
```python
import math

import jax
import jax.numpy as jnp
from jax import lax
from jax.sharding import PartitionSpec as P

TICKS = 2


def passed_along(array, axis, by):
    length = lax.axis_size(axis)
    return lax.ppermute(array, axis, [(i, (i + by) % length) for i in range(length)])


def row_positions(rows, tok_rows, ctx_count):
    half = tok_rows // 2
    block = rows // tok_rows
    offset = rows % tok_rows
    return jnp.where(
        offset < half, block * half + offset, (2 * ctx_count - 1 - block) * half + offset - half
    )


def pick_layer(norm_gain, w_query, w_keyval, w_out, layer):
    return tuple(
        (
            lax.dynamic_index_in_dim(stacked[0], layer, 0, keepdims=False)
            for stacked in (norm_gain, w_query, w_keyval, w_out)
        )
    )


def update_stats(stats, block, key_pos, queries, query_pos, query_seg, segment_ids):
    running_max, running_sum, weighted = stats
    head_dim = queries.shape[-1]
    key_part = block[..., :head_dim]
    value_part = block[..., head_dim:]
    scores = jnp.einsum("sqhd,skd->sqhk", queries, key_part, preferred_element_type=jnp.float32)
    scores = scores * (1.0 / math.sqrt(head_dim))
    key_seg = jnp.take(segment_ids, key_pos, axis=1)
    allowed = (key_pos[None, None, :] <= query_pos[None, :, None]) & (
        key_seg[:, None, :] == query_seg[:, :, None]
    )
    allowed = allowed[:, :, None, :]
    scores = jnp.where(allowed, scores, -1e30)
    new_max = jnp.maximum(running_max, jnp.max(scores, axis=-1))
    expon = jnp.where(allowed, jnp.exp(scores - new_max[..., None]), 0.0)
    factor = jnp.exp(running_max - new_max)
    running_sum = running_sum * factor + jnp.sum(expon, axis=-1)
    weighted = weighted * factor[..., None] + jnp.einsum(
        "sqhk,skd->sqhd", expon.astype(jnp.bfloat16), value_part, preferred_element_type=jnp.float32
    )
    return (new_max, running_sum, weighted)


def attend(queries, keyvals, query_pos, query_seg, segment_ids, ctx_index, ctx_count, tok_rows):
    seqs_here, rows_here, head_count, head_dim = queries.shape
    init = (
        jnp.full((seqs_here, rows_here, head_count), -1e30, jnp.float32),
        jnp.zeros((seqs_here, rows_here, head_count), jnp.float32),
        jnp.zeros((seqs_here, rows_here, head_count, head_dim), jnp.float32),
    )

    def cycle_turn(cycle_step, carry):
        stats, block = carry
        source = (ctx_index - cycle_step) % ctx_count
        key_pos = row_positions(
            source * tok_rows + lax.iota(jnp.int32, tok_rows), tok_rows, ctx_count
        )
        stats = update_stats(stats, block, key_pos, queries, query_pos, query_seg, segment_ids)
        block = passed_along(block, "ctx", 1)
        return (stats, block)

    stats, block = lax.fori_loop(0, ctx_count - 1, cycle_turn, (init, keyvals))
    last_source = (ctx_index - (ctx_count - 1)) % ctx_count
    last_pos = row_positions(
        last_source * tok_rows + lax.iota(jnp.int32, tok_rows), tok_rows, ctx_count
    )
    stats = update_stats(stats, block, last_pos, queries, query_pos, query_seg, segment_ids)
    running_max, running_sum, weighted = stats
    attended = (weighted / running_sum[..., None]).astype(jnp.bfloat16)
    return attended.reshape(seqs_here * rows_here, head_count * head_dim)


def body(activations, norm_gain, w_query, w_keyval, w_out, segment_ids, layer_order):
    ctx_count = lax.axis_size("ctx")
    ctx_index = lax.axis_index("ctx")
    state = activations[0]
    seqs_here, tok_rows, model_width = state.shape
    query_width = w_query.shape[-1]
    kv_width = w_keyval.shape[-1]
    head_dim = kv_width // 2
    head_count = query_width // head_dim
    query_pos = row_positions(
        ctx_index * tok_rows + lax.iota(jnp.int32, tok_rows), tok_rows, ctx_count
    )
    query_seg = jnp.take(segment_ids, query_pos, axis=1)
    shards = []
    for tick_index in range(TICKS):
        shards.append(pick_layer(norm_gain, w_query, w_keyval, w_out, layer_order[tick_index, 0]))
    for tick_index in range(TICKS):
        flat = state.reshape(seqs_here * tok_rows, model_width)
        scaled = flat * lax.rsqrt(jnp.mean(flat * flat, axis=1, keepdims=True) + 1e-05)
        gain_part, query_part, keyval_part, out_part = shards[tick_index]
        gain_piece = lax.all_gather(gain_part, "ctx", axis=0, tiled=True)
        query_piece = lax.all_gather(query_part, "ctx", axis=0, tiled=True)
        keyval_piece = lax.all_gather(keyval_part, "ctx", axis=0, tiled=True)
        hidden_piece = (scaled * gain_piece.astype(jnp.float32)[None, :]).astype(jnp.bfloat16)
        query_sum = jnp.dot(hidden_piece, query_piece, preferred_element_type=jnp.float32)
        keyval_sum = jnp.dot(hidden_piece, keyval_piece, preferred_element_type=jnp.float32)
        queries = query_sum.astype(jnp.bfloat16).reshape(seqs_here, tok_rows, head_count, head_dim)
        keyvals = keyval_sum.astype(jnp.bfloat16).reshape(seqs_here, tok_rows, kv_width)
        attended = attend(
            queries, keyvals, query_pos, query_seg, segment_ids, ctx_index, ctx_count, tok_rows
        )
        mixed = jnp.dot(
            attended,
            lax.all_gather(out_part, "ctx", axis=1, tiled=True),
            preferred_element_type=jnp.float32,
        )
        state = (flat + mixed).reshape(seqs_here, tok_rows, model_width)
        state = passed_along(state.astype(jnp.bfloat16), "pipe", 1).astype(state.dtype)
    return state[None]


def solution(mesh):
    in_specs = (
        P("pipe", None, "ctx", None),
        P("pipe", None, "ctx"),
        P("pipe", None, "ctx", None),
        P("pipe", None, "ctx", None),
        P("pipe", None, None, "ctx"),
        P(),
        P(None, "pipe"),
    )
    out_specs = P("pipe", None, "ctx", None)
    return jax.shard_map(body, mesh=mesh, in_specs=in_specs, out_specs=out_specs, check_vma=False)
```

profile of v0, /device:TPU:0, one launch (start us, length us, event | category | flops | bytes accessed | tf_op | source)
XLA Modules:
  0.0 537.5 jit_solution(4945558084599598163)
XLA Ops:
  20.1 42.4 %all-gather = bf16[1,1,4096]{2,1,0:T(2,128)(2,1)S(1)} all-gather(bf16[1,1,256]{2,1,0:T(2,128)(2,1)S(1)} %get-tuple-element.759), channel_id=2, replica_groups=mesh['ctx'=16,'pipe'=2] {'ctx'}, dimensions={2}, use_global_device_ids=true | all-gather | bytes 8704 | tf_op jit(solution)/shard_map/all_gather | solution.py:106
  64.1 13.2 %all-gather.15.cloned.1.call-done = bf16[1,1,4096,256]{3,2,1,0:T(8,128)(2,1)} async-done(((bf16[1,1,256,256]{3,2,1,0:T(8,128)(2,1)}), bf16[1,1,4096,256]{3,2,1,0:T(8,128)(2,1)}) %all-gather.15.cloned.1.call-update) | async-done | bytes 2097168 | tf_op jit(solution)/shard_map/all_gather | solution.py:108
  79.4 75.4 %all-gather.17.cloned.1.call-done = bf16[1,1,4096,512]{3,2,1,0:T(8,128)(2,1)} async-done(((bf16[1,1,256,512]{3,2,1,0:T(8,128)(2,1)}), bf16[1,1,4096,512]{3,2,1,0:T(8,128)(2,1)}) %all-gather.17.cloned.1.call-update) | async-done | bytes 4194320 | tf_op jit(solution)/shard_map/all_gather | solution.py:107
  157.8 127.8 %while.46 = (s32[]{:T(128)}, f32[1,128,4]{1,2,0:T(4,128)S(1)}, f32[1,128,4]{1,2,0:T(4,128)S(1)}, f32[1,128,4,128]{3,1,2,0:T(8,128)S(1)}, bf16[1,128,256]{2,1,0:T...) while((s32[]{:T(128)}, f32[1,128,4]{1,2,0:T(4,128)S(1)}, ...), condition=%wide.region_4.6_spmd.clone, body=%wide.region_1.5_spmd.clone.sunk | while | flops 34406160 | bytes 2009938 | solution.py:75
  175.6 6.2 %collective-permute-done = bf16[1,128,256]{2,1,0:T(8,128)(2,1)S(1)} collective-permute-done((bf16[1,128,256]{2,1,0:T(8,128)(2,1)S(1)}, bf16[1,128,256]{2,1,0:T(8,128)(2,1)S(1)}, u32[]{:S(2)}, u32[]{:S(2)}) %collective-permute-start) | collective-permute-done | bytes 65568 | tf_op jit(solution)/shard_map/while/body/eval_jaxpr/ppermute | solution.py:13
  183.9 6.0 %collective-permute-done = bf16[1,128,256]{2,1,0:T(8,128)(2,1)S(1)} collective-permute-done((bf16[1,128,256]{2,1,0:T(8,128)(2,1)S(1)}, bf16[1,128,256]{2,1,0:T(8,128)(2,1)S(1)}, u32[]{:S(2)}, u32[]{:S(2)}) %collective-permute-start) | collective-permute-done | bytes 65568 | tf_op jit(solution)/shard_map/while/body/eval_jaxpr/ppermute | solution.py:13
  191.9 6.5 %collective-permute-done = bf16[1,128,256]{2,1,0:T(8,128)(2,1)S(1)} collective-permute-done((bf16[1,128,256]{2,1,0:T(8,128)(2,1)S(1)}, bf16[1,128,256]{2,1,0:T(8,128)(2,1)S(1)}, u32[]{:S(2)}, u32[]{:S(2)}) %collective-permute-start) | collective-permute-done | bytes 65568 | tf_op jit(solution)/shard_map/while/body/eval_jaxpr/ppermute | solution.py:13
  200.4 6.0 %collective-permute-done = bf16[1,128,256]{2,1,0:T(8,128)(2,1)S(1)} collective-permute-done((bf16[1,128,256]{2,1,0:T(8,128)(2,1)S(1)}, bf16[1,128,256]{2,1,0:T(8,128)(2,1)S(1)}, u32[]{:S(2)}, u32[]{:S(2)}) %collective-permute-start) | collective-permute-done | bytes 65568 | tf_op jit(solution)/shard_map/while/body/eval_jaxpr/ppermute | solution.py:13
  208.4 7.2 %collective-permute-done = bf16[1,128,256]{2,1,0:T(8,128)(2,1)S(1)} collective-permute-done((bf16[1,128,256]{2,1,0:T(8,128)(2,1)S(1)}, bf16[1,128,256]{2,1,0:T(8,128)(2,1)S(1)}, u32[]{:S(2)}, u32[]{:S(2)}) %collective-permute-start) | collective-permute-done | bytes 65568 | tf_op jit(solution)/shard_map/while/body/eval_jaxpr/ppermute | solution.py:13
  217.6 7.3 %collective-permute-done = bf16[1,128,256]{2,1,0:T(8,128)(2,1)S(1)} collective-permute-done((bf16[1,128,256]{2,1,0:T(8,128)(2,1)S(1)}, bf16[1,128,256]{2,1,0:T(8,128)(2,1)S(1)}, u32[]{:S(2)}, u32[]{:S(2)}) %collective-permute-start) | collective-permute-done | bytes 65568 | tf_op jit(solution)/shard_map/while/body/eval_jaxpr/ppermute | solution.py:13
  226.9 7.3 %collective-permute-done = bf16[1,128,256]{2,1,0:T(8,128)(2,1)S(1)} collective-permute-done((bf16[1,128,256]{2,1,0:T(8,128)(2,1)S(1)}, bf16[1,128,256]{2,1,0:T(8,128)(2,1)S(1)}, u32[]{:S(2)}, u32[]{:S(2)}) %collective-permute-start) | collective-permute-done | bytes 65568 | tf_op jit(solution)/shard_map/while/body/eval_jaxpr/ppermute | solution.py:13
  236.2 7.3 %collective-permute-done = bf16[1,128,256]{2,1,0:T(8,128)(2,1)S(1)} collective-permute-done((bf16[1,128,256]{2,1,0:T(8,128)(2,1)S(1)}, bf16[1,128,256]{2,1,0:T(8,128)(2,1)S(1)}, u32[]{:S(2)}, u32[]{:S(2)}) %collective-permute-start) | collective-permute-done | bytes 65568 | tf_op jit(solution)/shard_map/while/body/eval_jaxpr/ppermute | solution.py:13
  245.6 7.2 %collective-permute-done = bf16[1,128,256]{2,1,0:T(8,128)(2,1)S(1)} collective-permute-done((bf16[1,128,256]{2,1,0:T(8,128)(2,1)S(1)}, bf16[1,128,256]{2,1,0:T(8,128)(2,1)S(1)}, u32[]{:S(2)}, u32[]{:S(2)}) %collective-permute-start) | collective-permute-done | bytes 65568 | tf_op jit(solution)/shard_map/while/body/eval_jaxpr/ppermute | solution.py:13
  254.8 5.9 %collective-permute-done = bf16[1,128,256]{2,1,0:T(8,128)(2,1)S(1)} collective-permute-done((bf16[1,128,256]{2,1,0:T(8,128)(2,1)S(1)}, bf16[1,128,256]{2,1,0:T(8,128)(2,1)S(1)}, u32[]{:S(2)}, u32[]{:S(2)}) %collective-permute-start) | collective-permute-done | bytes 65568 | tf_op jit(solution)/shard_map/while/body/eval_jaxpr/ppermute | solution.py:13
  262.7 6.3 %collective-permute-done = bf16[1,128,256]{2,1,0:T(8,128)(2,1)S(1)} collective-permute-done((bf16[1,128,256]{2,1,0:T(8,128)(2,1)S(1)}, bf16[1,128,256]{2,1,0:T(8,128)(2,1)S(1)}, u32[]{:S(2)}, u32[]{:S(2)}) %collective-permute-start) | collective-permute-done | bytes 65568 | tf_op jit(solution)/shard_map/while/body/eval_jaxpr/ppermute | solution.py:13
  271.0 6.6 %collective-permute-done = bf16[1,128,256]{2,1,0:T(8,128)(2,1)S(1)} collective-permute-done((bf16[1,128,256]{2,1,0:T(8,128)(2,1)S(1)}, bf16[1,128,256]{2,1,0:T(8,128)(2,1)S(1)}, u32[]{:S(2)}, u32[]{:S(2)}) %collective-permute-start) | collective-permute-done | bytes 65568 | tf_op jit(solution)/shard_map/while/body/eval_jaxpr/ppermute | solution.py:13
  279.6 6.0 %collective-permute-done = bf16[1,128,256]{2,1,0:T(8,128)(2,1)S(1)} collective-permute-done((bf16[1,128,256]{2,1,0:T(8,128)(2,1)S(1)}, bf16[1,128,256]{2,1,0:T(8,128)(2,1)S(1)}, u32[]{:S(2)}, u32[]{:S(2)}) %collective-permute-start) | collective-permute-done | bytes 65568 | tf_op jit(solution)/shard_map/while/body/eval_jaxpr/ppermute | solution.py:13
  289.6 35.9 %all-gather.4 = bf16[1,1,4096]{2,1,0:T(2,128)(2,1)S(1)} all-gather(bf16[1,1,256]{2,1,0:T(2,128)(2,1)S(1)} %get-tuple-element.758), channel_id=6, replica_groups=mesh['ctx'=16,'pipe'=2] {'ctx'}, dimensions={2}, use_global_device_ids=true | all-gather | bytes 8704 | tf_op jit(solution)/shard_map/all_gather | solution.py:106
  333.9 59.0 %all-gather.21.cloned.1.call-done = bf16[1,1,4096,256]{3,2,1,0:T(8,128)(2,1)} async-done(((bf16[1,1,256,256]{3,2,1,0:T(8,128)(2,1)}), bf16[1,1,4096,256]{3,2,1,0:T(8,128)(2,1)}) %all-gather.21.cloned.1.call-update) | async-done | bytes 2097168 | tf_op jit(solution)/shard_map/all_gather | solution.py:108
  395.1 127.5 %while.47 = (s32[]{:T(128)}, f32[1,128,4]{1,2,0:T(4,128)S(1)}, f32[1,128,4]{1,2,0:T(4,128)S(1)}, f32[1,128,4,128]{3,1,2,0:T(8,128)S(1)}, bf16[1,128,256]{2,1,0:T...) while((s32[]{:T(128)}, f32[1,128,4]{1,2,0:T(4,128)S(1)}, ...), condition=%wide.region_11.13_spmd.clone, body=%wide.region_8.12_spmd.clone.sunk | while | flops 34406160 | bytes 2009938 | solution.py:75
  405.0 6.4 %collective-permute-done.1 = bf16[1,128,256]{2,1,0:T(8,128)(2,1)S(1)} collective-permute-done((bf16[1,128,256]{2,1,0:T(8,128)(2,1)S(1)}, bf16[1,128,256]{2,1,0:T(8,128)(2,1)S(1)}, u32[]{:S(2)}, u32[]{:S(2)}) %collective-permute-start.1) | collective-permute-done | bytes 65568 | tf_op jit(solution)/shard_map/while/body/eval_jaxpr/ppermute | solution.py:13
  413.4 6.3 %collective-permute-done.1 = bf16[1,128,256]{2,1,0:T(8,128)(2,1)S(1)} collective-permute-done((bf16[1,128,256]{2,1,0:T(8,128)(2,1)S(1)}, bf16[1,128,256]{2,1,0:T(8,128)(2,1)S(1)}, u32[]{:S(2)}, u32[]{:S(2)}) %collective-permute-start.1) | collective-permute-done | bytes 65568 | tf_op jit(solution)/shard_map/while/body/eval_jaxpr/ppermute | solution.py:13
  421.7 6.1 %collective-permute-done.1 = bf16[1,128,256]{2,1,0:T(8,128)(2,1)S(1)} collective-permute-done((bf16[1,128,256]{2,1,0:T(8,128)(2,1)S(1)}, bf16[1,128,256]{2,1,0:T(8,128)(2,1)S(1)}, u32[]{:S(2)}, u32[]{:S(2)}) %collective-permute-start.1) | collective-permute-done | bytes 65568 | tf_op jit(solution)/shard_map/while/body/eval_jaxpr/ppermute | solution.py:13
  429.8 6.3 %collective-permute-done.1 = bf16[1,128,256]{2,1,0:T(8,128)(2,1)S(1)} collective-permute-done((bf16[1,128,256]{2,1,0:T(8,128)(2,1)S(1)}, bf16[1,128,256]{2,1,0:T(8,128)(2,1)S(1)}, u32[]{:S(2)}, u32[]{:S(2)}) %collective-permute-start.1) | collective-permute-done | bytes 65568 | tf_op jit(solution)/shard_map/while/body/eval_jaxpr/ppermute | solution.py:13
  445.9 7.4 %collective-permute-done.1 = bf16[1,128,256]{2,1,0:T(8,128)(2,1)S(1)} collective-permute-done((bf16[1,128,256]{2,1,0:T(8,128)(2,1)S(1)}, bf16[1,128,256]{2,1,0:T(8,128)(2,1)S(1)}, u32[]{:S(2)}, u32[]{:S(2)}) %collective-permute-start.1) | collective-permute-done | bytes 65568 | tf_op jit(solution)/shard_map/while/body/eval_jaxpr/ppermute | solution.py:13
  455.4 7.6 %collective-permute-done.1 = bf16[1,128,256]{2,1,0:T(8,128)(2,1)S(1)} collective-permute-done((bf16[1,128,256]{2,1,0:T(8,128)(2,1)S(1)}, bf16[1,128,256]{2,1,0:T(8,128)(2,1)S(1)}, u32[]{:S(2)}, u32[]{:S(2)}) %collective-permute-start.1) | collective-permute-done | bytes 65568 | tf_op jit(solution)/shard_map/while/body/eval_jaxpr/ppermute | solution.py:13
  465.0 7.3 %collective-permute-done.1 = bf16[1,128,256]{2,1,0:T(8,128)(2,1)S(1)} collective-permute-done((bf16[1,128,256]{2,1,0:T(8,128)(2,1)S(1)}, bf16[1,128,256]{2,1,0:T(8,128)(2,1)S(1)}, u32[]{:S(2)}, u32[]{:S(2)}) %collective-permute-start.1) | collective-permute-done | bytes 65568 | tf_op jit(solution)/shard_map/while/body/eval_jaxpr/ppermute | solution.py:13
  474.3 7.2 %collective-permute-done.1 = bf16[1,128,256]{2,1,0:T(8,128)(2,1)S(1)} collective-permute-done((bf16[1,128,256]{2,1,0:T(8,128)(2,1)S(1)}, bf16[1,128,256]{2,1,0:T(8,128)(2,1)S(1)}, u32[]{:S(2)}, u32[]{:S(2)}) %collective-permute-start.1) | collective-permute-done | bytes 65568 | tf_op jit(solution)/shard_map/while/body/eval_jaxpr/ppermute | solution.py:13
  483.5 7.2 %collective-permute-done.1 = bf16[1,128,256]{2,1,0:T(8,128)(2,1)S(1)} collective-permute-done((bf16[1,128,256]{2,1,0:T(8,128)(2,1)S(1)}, bf16[1,128,256]{2,1,0:T(8,128)(2,1)S(1)}, u32[]{:S(2)}, u32[]{:S(2)}) %collective-permute-start.1) | collective-permute-done | bytes 65568 | tf_op jit(solution)/shard_map/while/body/eval_jaxpr/ppermute | solution.py:13
  492.8 5.9 %collective-permute-done.1 = bf16[1,128,256]{2,1,0:T(8,128)(2,1)S(1)} collective-permute-done((bf16[1,128,256]{2,1,0:T(8,128)(2,1)S(1)}, bf16[1,128,256]{2,1,0:T(8,128)(2,1)S(1)}, u32[]{:S(2)}, u32[]{:S(2)}) %collective-permute-start.1) | collective-permute-done | bytes 65568 | tf_op jit(solution)/shard_map/while/body/eval_jaxpr/ppermute | solution.py:13
  500.6 6.2 %collective-permute-done.1 = bf16[1,128,256]{2,1,0:T(8,128)(2,1)S(1)} collective-permute-done((bf16[1,128,256]{2,1,0:T(8,128)(2,1)S(1)}, bf16[1,128,256]{2,1,0:T(8,128)(2,1)S(1)}, u32[]{:S(2)}, u32[]{:S(2)}) %collective-permute-start.1) | collective-permute-done | bytes 65568 | tf_op jit(solution)/shard_map/while/body/eval_jaxpr/ppermute | solution.py:13
  508.9 5.9 %collective-permute-done.1 = bf16[1,128,256]{2,1,0:T(8,128)(2,1)S(1)} collective-permute-done((bf16[1,128,256]{2,1,0:T(8,128)(2,1)S(1)}, bf16[1,128,256]{2,1,0:T(8,128)(2,1)S(1)}, u32[]{:S(2)}, u32[]{:S(2)}) %collective-permute-start.1) | collective-permute-done | bytes 65568 | tf_op jit(solution)/shard_map/while/body/eval_jaxpr/ppermute | solution.py:13
  (502 shorter events, 125.2 us)
Async XLA Ops:
  6.5 70.8 %all-gather.15.cloned.1.call-start = ((), (), s32[]{:S(2)}) async-start(), calls=%async_computation | async-start | bytes 2228224 | tf_op jit(solution)/shard_map/all_gather | solution.py:108
  13.6 141.2 %all-gather.17.cloned.1.call-start = ((), (), s32[]{:S(2)}) async-start(), calls=%async_computation.1 | async-start | bytes 4456448 | tf_op jit(solution)/shard_map/all_gather | solution.py:107
  15.6 270.9 %all-gather.19.cloned.1.call-start = ((), (), s32[]{:S(2)}) async-start(), calls=%async_computation.2 | async-start | bytes 4456448 | tf_op jit(solution)/shard_map/all_gather | solution.py:119
  17.5 313.4 %all-gather.23.cloned.1.call-start = ((), (), s32[]{:S(2)}) async-start(), calls=%async_computation.4 | async-start | bytes 4456448 | tf_op jit(solution)/shard_map/all_gather | solution.py:107
  18.1 374.9 %all-gather.21.cloned.1.call-start = ((), (), s32[]{:S(2)}) async-start(), calls=%async_computation.3 | async-start | bytes 2228224 | tf_op jit(solution)/shard_map/all_gather | solution.py:108
  18.7 504.7 %all-gather.25.cloned.1.call-start = ((), (), s32[]{:S(2)}) async-start(), calls=%async_computation.5 | async-start | bytes 4456448 | tf_op jit(solution)/shard_map/all_gather | solution.py:119
  157.9 7.9 %collective-permute-start = (bf16[1,128,256]{2,1,0:T(8,128)(2,1)S(1)}, bf16[1,128,256]{2,1,0:T(8,128)(2,1)S(1)}, u32[]{:S(2)}, u32[]{:S(2)}) collective-permute-start(bf16[1,128,256]{2,1,0:T(8,128)(2,1)S(1)} %copy.59), channel_id=1, source_target_pairs={{0,2},{2,4},{4,6},{6,8},{8,10},{10,12},{12,14},{14,16},{16,18},{18... | collective-permute-start | bytes 196616 | tf_op jit(solution)/shard_map/while/body/eval_jaxpr/ppermute | solution.py:13
  173.7 8.2 %collective-permute-start = (bf16[1,128,256]{2,1,0:T(8,128)(2,1)S(1)}, bf16[1,128,256]{2,1,0:T(8,128)(2,1)S(1)}, u32[]{:S(2)}, u32[]{:S(2)}) collective-permute-start(bf16[1,128,256]{2,1,0:T(8,128)(2,1)S(1)} %copy.59), channel_id=1, source_target_pairs={{0,2},{2,4},{4,6},{6,8},{8,10},{10,12},{12,14},{14,16},{16,18},{18... | collective-permute-start | bytes 196616 | tf_op jit(solution)/shard_map/while/body/eval_jaxpr/ppermute | solution.py:13
  181.9 8.0 %collective-permute-start = (bf16[1,128,256]{2,1,0:T(8,128)(2,1)S(1)}, bf16[1,128,256]{2,1,0:T(8,128)(2,1)S(1)}, u32[]{:S(2)}, u32[]{:S(2)}) collective-permute-start(bf16[1,128,256]{2,1,0:T(8,128)(2,1)S(1)} %copy.59), channel_id=1, source_target_pairs={{0,2},{2,4},{4,6},{6,8},{8,10},{10,12},{12,14},{14,16},{16,18},{18... | collective-permute-start | bytes 196616 | tf_op jit(solution)/shard_map/while/body/eval_jaxpr/ppermute | solution.py:13
  189.9 8.5 %collective-permute-start = (bf16[1,128,256]{2,1,0:T(8,128)(2,1)S(1)}, bf16[1,128,256]{2,1,0:T(8,128)(2,1)S(1)}, u32[]{:S(2)}, u32[]{:S(2)}) collective-permute-start(bf16[1,128,256]{2,1,0:T(8,128)(2,1)S(1)} %copy.59), channel_id=1, source_target_pairs={{0,2},{2,4},{4,6},{6,8},{8,10},{10,12},{12,14},{14,16},{16,18},{18... | collective-permute-start | bytes 196616 | tf_op jit(solution)/shard_map/while/body/eval_jaxpr/ppermute | solution.py:13
  198.4 7.9 %collective-permute-start = (bf16[1,128,256]{2,1,0:T(8,128)(2,1)S(1)}, bf16[1,128,256]{2,1,0:T(8,128)(2,1)S(1)}, u32[]{:S(2)}, u32[]{:S(2)}) collective-permute-start(bf16[1,128,256]{2,1,0:T(8,128)(2,1)S(1)} %copy.59), channel_id=1, source_target_pairs={{0,2},{2,4},{4,6},{6,8},{8,10},{10,12},{12,14},{14,16},{16,18},{18... | collective-permute-start | bytes 196616 | tf_op jit(solution)/shard_map/while/body/eval_jaxpr/ppermute | solution.py:13
  206.4 9.2 %collective-permute-start = (bf16[1,128,256]{2,1,0:T(8,128)(2,1)S(1)}, bf16[1,128,256]{2,1,0:T(8,128)(2,1)S(1)}, u32[]{:S(2)}, u32[]{:S(2)}) collective-permute-start(bf16[1,128,256]{2,1,0:T(8,128)(2,1)S(1)} %copy.59), channel_id=1, source_target_pairs={{0,2},{2,4},{4,6},{6,8},{8,10},{10,12},{12,14},{14,16},{16,18},{18... | collective-permute-start | bytes 196616 | tf_op jit(solution)/shard_map/while/body/eval_jaxpr/ppermute | solution.py:13
  215.6 9.3 %collective-permute-start = (bf16[1,128,256]{2,1,0:T(8,128)(2,1)S(1)}, bf16[1,128,256]{2,1,0:T(8,128)(2,1)S(1)}, u32[]{:S(2)}, u32[]{:S(2)}) collective-permute-start(bf16[1,128,256]{2,1,0:T(8,128)(2,1)S(1)} %copy.59), channel_id=1, source_target_pairs={{0,2},{2,4},{4,6},{6,8},{8,10},{10,12},{12,14},{14,16},{16,18},{18... | collective-permute-start | bytes 196616 | tf_op jit(solution)/shard_map/while/body/eval_jaxpr/ppermute | solution.py:13
  224.9 9.3 %collective-permute-start = (bf16[1,128,256]{2,1,0:T(8,128)(2,1)S(1)}, bf16[1,128,256]{2,1,0:T(8,128)(2,1)S(1)}, u32[]{:S(2)}, u32[]{:S(2)}) collective-permute-start(bf16[1,128,256]{2,1,0:T(8,128)(2,1)S(1)} %copy.59), channel_id=1, source_target_pairs={{0,2},{2,4},{4,6},{6,8},{8,10},{10,12},{12,14},{14,16},{16,18},{18... | collective-permute-start | bytes 196616 | tf_op jit(solution)/shard_map/while/body/eval_jaxpr/ppermute | solution.py:13
  234.2 9.3 %collective-permute-start = (bf16[1,128,256]{2,1,0:T(8,128)(2,1)S(1)}, bf16[1,128,256]{2,1,0:T(8,128)(2,1)S(1)}, u32[]{:S(2)}, u32[]{:S(2)}) collective-permute-start(bf16[1,128,256]{2,1,0:T(8,128)(2,1)S(1)} %copy.59), channel_id=1, source_target_pairs={{0,2},{2,4},{4,6},{6,8},{8,10},{10,12},{12,14},{14,16},{16,18},{18... | collective-permute-start | bytes 196616 | tf_op jit(solution)/shard_map/while/body/eval_jaxpr/ppermute | solution.py:13
  243.6 9.2 %collective-permute-start = (bf16[1,128,256]{2,1,0:T(8,128)(2,1)S(1)}, bf16[1,128,256]{2,1,0:T(8,128)(2,1)S(1)}, u32[]{:S(2)}, u32[]{:S(2)}) collective-permute-start(bf16[1,128,256]{2,1,0:T(8,128)(2,1)S(1)} %copy.59), channel_id=1, source_target_pairs={{0,2},{2,4},{4,6},{6,8},{8,10},{10,12},{12,14},{14,16},{16,18},{18... | collective-permute-start | bytes 196616 | tf_op jit(solution)/shard_map/while/body/eval_jaxpr/ppermute | solution.py:13
  252.8 7.9 %collective-permute-start = (bf16[1,128,256]{2,1,0:T(8,128)(2,1)S(1)}, bf16[1,128,256]{2,1,0:T(8,128)(2,1)S(1)}, u32[]{:S(2)}, u32[]{:S(2)}) collective-permute-start(bf16[1,128,256]{2,1,0:T(8,128)(2,1)S(1)} %copy.59), channel_id=1, source_target_pairs={{0,2},{2,4},{4,6},{6,8},{8,10},{10,12},{12,14},{14,16},{16,18},{18... | collective-permute-start | bytes 196616 | tf_op jit(solution)/shard_map/while/body/eval_jaxpr/ppermute | solution.py:13
  260.7 8.3 %collective-permute-start = (bf16[1,128,256]{2,1,0:T(8,128)(2,1)S(1)}, bf16[1,128,256]{2,1,0:T(8,128)(2,1)S(1)}, u32[]{:S(2)}, u32[]{:S(2)}) collective-permute-start(bf16[1,128,256]{2,1,0:T(8,128)(2,1)S(1)} %copy.59), channel_id=1, source_target_pairs={{0,2},{2,4},{4,6},{6,8},{8,10},{10,12},{12,14},{14,16},{16,18},{18... | collective-permute-start | bytes 196616 | tf_op jit(solution)/shard_map/while/body/eval_jaxpr/ppermute | solution.py:13
  269.0 8.6 %collective-permute-start = (bf16[1,128,256]{2,1,0:T(8,128)(2,1)S(1)}, bf16[1,128,256]{2,1,0:T(8,128)(2,1)S(1)}, u32[]{:S(2)}, u32[]{:S(2)}) collective-permute-start(bf16[1,128,256]{2,1,0:T(8,128)(2,1)S(1)} %copy.59), channel_id=1, source_target_pairs={{0,2},{2,4},{4,6},{6,8},{8,10},{10,12},{12,14},{14,16},{16,18},{18... | collective-permute-start | bytes 196616 | tf_op jit(solution)/shard_map/while/body/eval_jaxpr/ppermute | solution.py:13
  277.6 8.0 %collective-permute-start = (bf16[1,128,256]{2,1,0:T(8,128)(2,1)S(1)}, bf16[1,128,256]{2,1,0:T(8,128)(2,1)S(1)}, u32[]{:S(2)}, u32[]{:S(2)}) collective-permute-start(bf16[1,128,256]{2,1,0:T(8,128)(2,1)S(1)} %copy.59), channel_id=1, source_target_pairs={{0,2},{2,4},{4,6},{6,8},{8,10},{10,12},{12,14},{14,16},{16,18},{18... | collective-permute-start | bytes 196616 | tf_op jit(solution)/shard_map/while/body/eval_jaxpr/ppermute | solution.py:13
  289.5 36.1 %collective-permute-start.2 = (bf16[1,128,4096]{2,1,0:T(8,128)(2,1)S(1)}, bf16[1,128,4096]{2,1,0:T(8,128)(2,1)S(1)}, u32[]{:S(2)}, u32[]{:S(2)}) collective-permute-start(bf16[1,128,4096]{2,1,0:T(8,128)(2,1)S(1)} %fusion.37), channel_id=1, source_target_pairs={{0,1},{1,0},{2,3},{3,2},{4,5},{5,4},{6,7},{7,6},{8,9},{9,8},{10,11... | collective-permute-start | bytes 3145736 | tf_op jit(solution)/shard_map/ppermute | solution.py:13
  395.1 7.9 %collective-permute-start.1 = (bf16[1,128,256]{2,1,0:T(8,128)(2,1)S(1)}, bf16[1,128,256]{2,1,0:T(8,128)(2,1)S(1)}, u32[]{:S(2)}, u32[]{:S(2)}) collective-permute-start(bf16[1,128,256]{2,1,0:T(8,128)(2,1)S(1)} %copy.74), channel_id=1, source_target_pairs={{0,2},{2,4},{4,6},{6,8},{8,10},{10,12},{12,14},{14,16},{16,18},{18... | collective-permute-start | bytes 196616 | tf_op jit(solution)/shard_map/while/body/eval_jaxpr/ppermute | solution.py:13
  403.0 8.4 %collective-permute-start.1 = (bf16[1,128,256]{2,1,0:T(8,128)(2,1)S(1)}, bf16[1,128,256]{2,1,0:T(8,128)(2,1)S(1)}, u32[]{:S(2)}, u32[]{:S(2)}) collective-permute-start(bf16[1,128,256]{2,1,0:T(8,128)(2,1)S(1)} %copy.74), channel_id=1, source_target_pairs={{0,2},{2,4},{4,6},{6,8},{8,10},{10,12},{12,14},{14,16},{16,18},{18... | collective-permute-start | bytes 196616 | tf_op jit(solution)/shard_map/while/body/eval_jaxpr/ppermute | solution.py:13
  411.4 8.3 %collective-permute-start.1 = (bf16[1,128,256]{2,1,0:T(8,128)(2,1)S(1)}, bf16[1,128,256]{2,1,0:T(8,128)(2,1)S(1)}, u32[]{:S(2)}, u32[]{:S(2)}) collective-permute-start(bf16[1,128,256]{2,1,0:T(8,128)(2,1)S(1)} %copy.74), channel_id=1, source_target_pairs={{0,2},{2,4},{4,6},{6,8},{8,10},{10,12},{12,14},{14,16},{16,18},{18... | collective-permute-start | bytes 196616 | tf_op jit(solution)/shard_map/while/body/eval_jaxpr/ppermute | solution.py:13
  419.7 8.0 %collective-permute-start.1 = (bf16[1,128,256]{2,1,0:T(8,128)(2,1)S(1)}, bf16[1,128,256]{2,1,0:T(8,128)(2,1)S(1)}, u32[]{:S(2)}, u32[]{:S(2)}) collective-permute-start(bf16[1,128,256]{2,1,0:T(8,128)(2,1)S(1)} %copy.74), channel_id=1, source_target_pairs={{0,2},{2,4},{4,6},{6,8},{8,10},{10,12},{12,14},{14,16},{16,18},{18... | collective-permute-start | bytes 196616 | tf_op jit(solution)/shard_map/while/body/eval_jaxpr/ppermute | solution.py:13
  427.8 8.3 %collective-permute-start.1 = (bf16[1,128,256]{2,1,0:T(8,128)(2,1)S(1)}, bf16[1,128,256]{2,1,0:T(8,128)(2,1)S(1)}, u32[]{:S(2)}, u32[]{:S(2)}) collective-permute-start(bf16[1,128,256]{2,1,0:T(8,128)(2,1)S(1)} %copy.74), channel_id=1, source_target_pairs={{0,2},{2,4},{4,6},{6,8},{8,10},{10,12},{12,14},{14,16},{16,18},{18... | collective-permute-start | bytes 196616 | tf_op jit(solution)/shard_map/while/body/eval_jaxpr/ppermute | solution.py:13
  443.9 9.4 %collective-permute-start.1 = (bf16[1,128,256]{2,1,0:T(8,128)(2,1)S(1)}, bf16[1,128,256]{2,1,0:T(8,128)(2,1)S(1)}, u32[]{:S(2)}, u32[]{:S(2)}) collective-permute-start(bf16[1,128,256]{2,1,0:T(8,128)(2,1)S(1)} %copy.74), channel_id=1, source_target_pairs={{0,2},{2,4},{4,6},{6,8},{8,10},{10,12},{12,14},{14,16},{16,18},{18... | collective-permute-start | bytes 196616 | tf_op jit(solution)/shard_map/while/body/eval_jaxpr/ppermute | solution.py:13
  453.4 9.6 %collective-permute-start.1 = (bf16[1,128,256]{2,1,0:T(8,128)(2,1)S(1)}, bf16[1,128,256]{2,1,0:T(8,128)(2,1)S(1)}, u32[]{:S(2)}, u32[]{:S(2)}) collective-permute-start(bf16[1,128,256]{2,1,0:T(8,128)(2,1)S(1)} %copy.74), channel_id=1, source_target_pairs={{0,2},{2,4},{4,6},{6,8},{8,10},{10,12},{12,14},{14,16},{16,18},{18... | collective-permute-start | bytes 196616 | tf_op jit(solution)/shard_map/while/body/eval_jaxpr/ppermute | solution.py:13
  463.0 9.3 %collective-permute-start.1 = (bf16[1,128,256]{2,1,0:T(8,128)(2,1)S(1)}, bf16[1,128,256]{2,1,0:T(8,128)(2,1)S(1)}, u32[]{:S(2)}, u32[]{:S(2)}) collective-permute-start(bf16[1,128,256]{2,1,0:T(8,128)(2,1)S(1)} %copy.74), channel_id=1, source_target_pairs={{0,2},{2,4},{4,6},{6,8},{8,10},{10,12},{12,14},{14,16},{16,18},{18... | collective-permute-start | bytes 196616 | tf_op jit(solution)/shard_map/while/body/eval_jaxpr/ppermute | solution.py:13
  472.3 9.2 %collective-permute-start.1 = (bf16[1,128,256]{2,1,0:T(8,128)(2,1)S(1)}, bf16[1,128,256]{2,1,0:T(8,128)(2,1)S(1)}, u32[]{:S(2)}, u32[]{:S(2)}) collective-permute-start(bf16[1,128,256]{2,1,0:T(8,128)(2,1)S(1)} %copy.74), channel_id=1, source_target_pairs={{0,2},{2,4},{4,6},{6,8},{8,10},{10,12},{12,14},{14,16},{16,18},{18... | collective-permute-start | bytes 196616 | tf_op jit(solution)/shard_map/while/body/eval_jaxpr/ppermute | solution.py:13
  481.5 9.2 %collective-permute-start.1 = (bf16[1,128,256]{2,1,0:T(8,128)(2,1)S(1)}, bf16[1,128,256]{2,1,0:T(8,128)(2,1)S(1)}, u32[]{:S(2)}, u32[]{:S(2)}) collective-permute-start(bf16[1,128,256]{2,1,0:T(8,128)(2,1)S(1)} %copy.74), channel_id=1, source_target_pairs={{0,2},{2,4},{4,6},{6,8},{8,10},{10,12},{12,14},{14,16},{16,18},{18... | collective-permute-start | bytes 196616 | tf_op jit(solution)/shard_map/while/body/eval_jaxpr/ppermute | solution.py:13
  498.6 8.2 %collective-permute-start.1 = (bf16[1,128,256]{2,1,0:T(8,128)(2,1)S(1)}, bf16[1,128,256]{2,1,0:T(8,128)(2,1)S(1)}, u32[]{:S(2)}, u32[]{:S(2)}) collective-permute-start(bf16[1,128,256]{2,1,0:T(8,128)(2,1)S(1)} %copy.74), channel_id=1, source_target_pairs={{0,2},{2,4},{4,6},{6,8},{8,10},{10,12},{12,14},{14,16},{16,18},{18... | collective-permute-start | bytes 196616 | tf_op jit(solution)/shard_map/while/body/eval_jaxpr/ppermute | solution.py:13
  (9 other events, 113.5 us)
Sparse Core Ops, SparseCore 0:
  13.7 63.4 all-gather.14
  80.1 74.7 all-gather.16
  157.6 88.6 all-gather.18
  248.8 82.0 all-gather.22
  333.5 59.3 all-gather.20
  395.5 88.5 all-gather.24
where the time goes:
time: 538 us; the launch traced here: 537 us
  waiting for transfers between devices  349 us (65%)
  blocking collectives  78.4 us (15%)
  local copies, waits for them, and re-layouts  44.6 us (8%)
  matrix products  31.5 us (6%)
  between operations  17.7 us (3%)
  other arithmetic  10.3 us (2%)
    ppermute x32, waiting for transfers between devices, passed_along(): lax.ppermute(array, axis, [(i, (i + by) % length) for i in range(length)])  195 us
    all_gather x2, waiting for transfers between devices, body(): query_piece = lax.all_gather(query_part, 'ctx', axis=0, tiled=True)  80.5 us
    all_gather x2, blocking collectives, body(): gain_piece = lax.all_gather(gain_part, 'ctx', axis=0, tiled=True)  78.4 us
    all_gather x2, waiting for transfers between devices, body(): keyval_piece = lax.all_gather(keyval_part, 'ctx', axis=0, tiled=True)  72.2 us
    gather x31, local copies, waits for them, and re-layouts, update_stats(): key_seg = jnp.take(segment_ids, key_pos, axis=1)  35.6 us
  transfers between devices with their start and end apart: 38, of which 35 were waited for; matrix products, arithmetic and copies ran while one was open for 15% of the time, Pallas kernels for 0%

commit v1 on v0

v1 whole, which is shorter than its diff:
```python
import functools
import itertools
import math

import jax
import jax.numpy as jnp
from jax import lax
from jax.experimental import pallas as pl
from jax.experimental.pallas import tpu as pltpu
from jax.sharding import PartitionSpec as P

TICKS = 2


def passed_along(array, axis, by):
    length = lax.axis_size(axis)
    return lax.ppermute(array, axis, [(i, (i + by) % length) for i in range(length)])


def grid_of(count):
    known = {16: (4, 2, 2), 32: (4, 8)}
    return known.get(count, (count,))


def orders_of(sizes):
    dims = tuple(range(len(sizes)))
    if len(dims) == 1:
        return (dims, dims)
    return (dims, dims[:-2] + (dims[-1], dims[-2]))


def gather_kernel(sizes, cuts, *refs):
    count = len(cuts)
    blocks, wholes = refs[:count], refs[count : 2 * count]
    send_sems, recv_sems, own_sems = refs[2 * count :]
    rank = len(sizes)
    strides = [math.prod(sizes[d + 1 :]) for d in range(rank)]
    me = lax.axis_index("ctx")
    coords = [(me // strides[d]) % sizes[d] for d in range(rank)]

    def place(delta):
        return sum(((coords[d] + delta[d]) % sizes[d]) * strides[d] for d in range(rank))

    def along(dim, by):
        return tuple(by if d == dim else 0 for d in range(rank))

    def flat(delta):
        return sum(delta[d] * strides[d] for d in range(rank))

    barrier = pltpu.get_barrier_semaphore()
    greeted = 0
    for dim in range(rank):
        for by in range(1, sizes[dim]):
            pl.semaphore_signal(
                barrier,
                inc=1,
                device_id={"ctx": place(along(dim, by))},
                device_id_type=pl.DeviceIdType.MESH,
            )
            greeted += 1
    pl.semaphore_wait(barrier, greeted)

    orders = orders_of(sizes)
    started = []
    used = {}

    def copy_of(which, part, delta, dim, by, send):
        rows = pl.ds(*cuts[which][part])
        source = place(delta)
        landing = wholes[which].at[source, rows]
        origin = landing if any(delta) else blocks[which].at[rows]
        seen = tuple((sizes[d] - by) % sizes[d] if d == dim else delta[d] for d in range(rank))
        return pltpu.make_async_remote_copy(
            src_ref=origin,
            dst_ref=landing,
            send_sem=send_sems.at[which, part, send],
            recv_sem=recv_sems.at[which, part, flat(seen)],
            device_id={"ctx": place(along(dim, by))},
            device_id_type=pl.DeviceIdType.MESH,
        )

    def pass_on(which, part, delta, phases):
        for phase in phases:
            dim = orders[part][phase]
            for by in range(1, sizes[dim]):
                send = used.get((which, part), 0)
                used[which, part] = send + 1
                copy = copy_of(which, part, delta, dim, by, send)
                copy.start()
                started.append(copy)

    def take(which, part, phase):
        order = orders[part]
        ranges = [range(1)] * rank
        for before in order[:phase]:
            ranges[before] = range(sizes[before])
        ranges[order[phase]] = range(1, sizes[order[phase]])
        for delta in itertools.product(*ranges):
            landing = wholes[which].at[place(delta), pl.ds(*cuts[which][part])]
            pltpu.make_async_remote_copy(
                src_ref=landing,
                dst_ref=landing,
                send_sem=send_sems.at[which, part, 0],
                recv_sem=recv_sems.at[which, part, flat(delta)],
                device_id={"ctx": place(along(order[phase], 1))},
                device_id_type=pl.DeviceIdType.MESH,
            ).wait_recv()
            pass_on(which, part, delta, range(phase + 1, rank))

    for which in range(count):
        for part in range(2):
            pass_on(which, part, (0,) * rank, range(rank))
    own = []
    for which in range(count):
        copy = pltpu.make_async_copy(blocks[which], wholes[which].at[me], own_sems.at[which])
        copy.start()
        own.append(copy)
    for turn in range(count + rank - 1):
        for which in range(count):
            phase = turn - which
            if 0 <= phase < rank:
                for part in range(2):
                    take(which, part, phase)
    for copy in own:
        copy.wait()
    for copy in started:
        copy.wait_send()


def gather_blocks(blocks, ctx_count, collective_id):
    cuts = []
    for block in blocks:
        rows = block.shape[0]
        first = rows // 32 * 16
        cuts.append(((0, first), (first, rows - first)))
    count = len(blocks)
    wholes = pl.pallas_call(
        functools.partial(gather_kernel, grid_of(ctx_count), tuple(cuts)),
        out_shape=[jax.ShapeDtypeStruct((ctx_count, *b.shape), b.dtype) for b in blocks],
        in_specs=[pl.BlockSpec(memory_space=pl.ANY)] * count,
        out_specs=[pl.BlockSpec(memory_space=pl.ANY)] * count,
        scratch_shapes=[
            pltpu.SemaphoreType.DMA((count, 2, ctx_count)),
            pltpu.SemaphoreType.DMA((count, 2, ctx_count)),
            pltpu.SemaphoreType.DMA((count,)),
        ],
        compiler_params=pltpu.CompilerParams(collective_id=collective_id, has_side_effects=True),
    )(*blocks)
    return wholes


def row_positions(rows, tok_rows, ctx_count):
    half = tok_rows // 2
    block = rows // tok_rows
    offset = rows % tok_rows
    return jnp.where(
        offset < half, block * half + offset, (2 * ctx_count - 1 - block) * half + offset - half
    )


def pick(stacked, layer):
    return lax.dynamic_index_in_dim(stacked[0], layer, 0, keepdims=False)


def attend(queries, keyvals, allowed):
    seqs_here, rows_here, head_count, head_dim = queries.shape
    keys = keyvals[..., :head_dim]
    values = keyvals[..., head_dim:]
    scores = jnp.einsum("sqhd,skd->shqk", queries, keys, preferred_element_type=jnp.float32)
    scores = scores * (1.0 / math.sqrt(head_dim))
    allowed = allowed[:, None]
    scores = jnp.where(allowed, scores, -1e30)
    top = jnp.max(scores, axis=-1, keepdims=True)
    probs = jnp.where(allowed, jnp.exp(scores - top), 0.0)
    totals = jnp.sum(probs, axis=-1)
    summed = jnp.einsum(
        "shqk,skd->sqhd", probs.astype(jnp.bfloat16), values, preferred_element_type=jnp.float32
    )
    attended = (summed / jnp.swapaxes(totals, 1, 2)[..., None]).astype(jnp.bfloat16)
    return attended.reshape(seqs_here * rows_here, head_count * head_dim)


def body(activations, norm_gain, w_query, w_keyval, w_out, segment_ids, layer_order):
    ctx_count = lax.axis_size("ctx")
    ctx_index = lax.axis_index("ctx")
    state = activations[0]
    seqs_here, tok_rows, model_width = state.shape
    query_width = w_query.shape[-1]
    kv_width = w_keyval.shape[-1]
    head_dim = kv_width // 2
    head_count = query_width // head_dim
    in_rows = w_query.shape[2]
    wide = query_width + kv_width
    in_parts, out_parts = [], []
    for tick in range(TICKS):
        layer = layer_order[tick, 0]
        gain_rows = jnp.pad(pick(norm_gain, layer)[None, :], ((0, 15), (0, wide - in_rows)))
        both = jnp.concatenate([pick(w_query, layer), pick(w_keyval, layer)], axis=1)
        in_parts.append(jnp.concatenate([both, gain_rows], axis=0))
        out_parts.append(pick(w_out, layer))
    wholes = gather_blocks(
        [part for pair in zip(in_parts, out_parts) for part in pair], ctx_count, 0
    )
    gathered = [(wholes[2 * tick], wholes[2 * tick + 1]) for tick in range(TICKS)]
    query_pos = row_positions(
        ctx_index * tok_rows + lax.iota(jnp.int32, tok_rows), tok_rows, ctx_count
    )
    query_seg = jnp.take(segment_ids, query_pos, axis=1)
    halves = segment_ids.reshape(seqs_here, 2, ctx_count, tok_rows // 2)
    by_row = jnp.stack([halves[:, 0], halves[:, 1, ::-1]], axis=2)
    key_seg = by_row.reshape(seqs_here, ctx_count * tok_rows)
    key_pos = row_positions(lax.iota(jnp.int32, ctx_count * tok_rows), tok_rows, ctx_count)
    allowed = (key_pos[None, None, :] <= query_pos[None, :, None]) & (
        key_seg[:, None, :] == query_seg[:, :, None]
    )
    for tick in range(TICKS):
        in_all, out_all = gathered[tick]
        flat = state.reshape(seqs_here * tok_rows, model_width)
        gain = in_all[:, in_rows, :in_rows].reshape(model_width)
        scaled = flat * lax.rsqrt(jnp.mean(flat * flat, axis=1, keepdims=True) + 1e-05)
        hidden = (scaled * gain.astype(jnp.float32)[None, :]).astype(jnp.bfloat16)
        sums = jnp.einsum(
            "tcd,cdw->tw",
            hidden.reshape(seqs_here * tok_rows, ctx_count, in_rows),
            in_all[:, :in_rows],
            preferred_element_type=jnp.float32,
        ).astype(jnp.bfloat16)
        queries = sums[:, :query_width].reshape(seqs_here, tok_rows, head_count, head_dim)
        (keyvals,) = gather_blocks([sums[:, query_width:]], ctx_count, 1)
        keyvals = keyvals.reshape(ctx_count, seqs_here, tok_rows, kv_width)
        keyvals = jnp.swapaxes(keyvals, 0, 1).reshape(seqs_here, ctx_count * tok_rows, kv_width)
        attended = attend(queries, keyvals, allowed)
        mixed = jnp.einsum(
            "tw,cwd->tcd", attended, out_all, preferred_element_type=jnp.float32
        ).reshape(flat.shape)
        state = (flat + mixed).reshape(seqs_here, tok_rows, model_width)
        state = passed_along(state.astype(jnp.bfloat16), "pipe", 1).astype(state.dtype)
    return state[None]


def solution(mesh):
    in_specs = (
        P("pipe", None, "ctx", None),
        P("pipe", None, "ctx"),
        P("pipe", None, "ctx", None),
        P("pipe", None, "ctx", None),
        P("pipe", None, None, "ctx"),
        P(),
        P(None, "pipe"),
    )
    out_specs = P("pipe", None, "ctx", None)
    return jax.shard_map(body, mesh=mesh, in_specs=in_specs, out_specs=out_specs, check_vma=False)
```

time: 538 us -> 297 us (0.55)
  waiting for transfers between devices: 349 us -> 2.65 us
  Pallas kernels: 0 us -> 236 us
  blocking collectives: 78.4 us -> 0 us
  local copies, waits for them, and re-layouts: 44.6 us -> 24.3 us
  between operations: 17.7 us -> 4.29 us
  matrix products: 31.5 us -> 20.8 us
    pallas_call x0 -> x3, Pallas kernels: none -> 236 us  [gather_blocks(): pl.pallas_call(functools.partial(gather_kernel, grid_of(ctx_count), tuple...]
    ppermute x32 -> x2, waiting for transfers between devices: 195 us -> 2.65 us  [passed_along(): lax.ppermute(array, axis, [(i, (i + by) % length) for i in range(length)])]
    all_gather x6 -> x0, waiting for transfers between devices: 153 us -> none  [the longest x2 80.5 us: body(): query_piece = lax.all_gather(query_part, 'ctx', axis=0, tiled=True)]
    all_gather x2 -> x0, blocking collectives: 78.4 us -> none  [body(): gain_piece = lax.all_gather(gain_part, 'ctx', axis=0, tiled=True)]
    gather x31 -> x0, local copies, waits for them, and re-layouts: 35.6 us -> none  [update_stats(): key_seg = jnp.take(segment_ids, key_pos, axis=1)]
    dot_general x0 -> x2, local copies, waits for them, and re-layouts: none -> 12.8 us  [body(): jnp.einsum('tw,cwd->tcd', attended, out_all, preferred_element_type=jnp.f...]
    dot_general x70 -> x8, matrix products: 31.5 us -> 20.8 us  [the longest x2 9.65 us: body(): jnp.einsum('tcd,cdw->tw', hidden.reshape(seqs_here * tok_rows, ctx_count,...]
  transfers between devices with their start and end apart: 38 -> 2, of which waited for: 35 -> 1; matrix products, arithmetic and copies ran while one was open for 15% -> 2% of each run, Pallas kernels for 0% -> 0%
where the time goes in v1:
time: 297 us
  Pallas kernels  236 us (79%)
  local copies, waits for them, and re-layouts  24.3 us (8%)
  matrix products  20.8 us (7%)
  other arithmetic  8.84 us (3%)
  between operations  4.29 us (1%)
    pallas_call x3, Pallas kernels, gather_blocks(): pl.pallas_call(functools.partial(gather_kernel, grid_of(ctx_count), tuple...  236 us
    dot_general x2, local copies, waits for them, and re-layouts, body(): jnp.einsum('tw,cwd->tcd', attended, out_all, preferred_element_type=jnp.f...  12.8 us
    dot_general x2, matrix products, body(): jnp.einsum('tcd,cdw->tw', hidden.reshape(seqs_here * tok_rows, ctx_count,...  9.65 us
  transfers between devices with their start and end apart: 2, of which 1 were waited for; matrix products, arithmetic and copies ran while one was open for 2% of the time, Pallas kernels for 0%

profile of v1, /device:TPU:0, one launch (start us, length us, event | category | flops | bytes accessed | tf_op | source)
XLA Modules:
  0.0 296.5 jit_solution(4514550751614461119)
XLA Ops:
  0.0 1.4 fusion.99
  5.5 1.1 dynamic-slice_bitcast_fusion.1
  6.5 1.0 dynamic-slice_bitcast_fusion.4
  7.5 0.8 fusion.90
  8.3 1.9 dynamic-slice_bitcast_fusion
  10.2 0.9 fusion.68
  11.1 186.9 %shard_map.73 = (bf16[16,272,768]{2,1,0:T(8,128)(2,1)}, bf16[16,512,256]{2,1,0:T(8,128)(2,1)}, bf16[16,272,768]{2,1,0:T(8,128)(2,1)}, bf16[16,512,256]{2,1,0:T(8,128)(2,1)}) custom-call(bf16[272,768]{1,0:T(8,128)(2,1)} %get-tuple-element.31.refs_0_, bf16[512,256]{1,0:T(8,128)(2,1)} %get-tuple-element.14.refs_1_, bf16[272,768]{1,0:T(8,128)(2,1)} %get-tuple-element.32.refs_2_, ...), custom_call_target="tpu_custom_call" | custom-call | tf_op jit(solution)/shard_map/pallas_call | solution.py:137
  198.0 0.9 slice_convert_fusion.1
  199.1 0.7 copy.37
  199.8 4.8 %fusion.37 = bf16[128,768]{1,0:T(8,128)(2,1)S(1)} fusion(bf16[16,272,768]{2,1,0:T(8,128)(2,1)} %get-tuple-element.9, f32[128,16,256]{2,1,0:T(8,128)S(1)} %bitcast.210, f32[16,256]{1,0:T(8,128)S(1)} %bitcast.220, f32[128]{0:T(128)S(1)} %add_rsqrt_fusion.1), kind=kOutput, calls=%fused_computation.40 | convolution fusion | flops 806977536 | bytes 8602112 | tf_op jit(solution)/shard_map/tcd,cdw->tw/dot_general | solution.py:222
  204.6 0.6 slice.66.refs_0_
  205.3 29.9 %shard_map.74 = bf16[16,128,256]{2,1,0:T(8,128)(2,1)} custom-call(bf16[128,256]{1,0:T(8,128)(2,1)} %slice.66.refs_0_), custom_call_target="tpu_custom_call" | custom-call | tf_op jit(solution)/shard_map/pallas_call | solution.py:137
  235.3 1.3 gather_fusion
  237.1 0.7 reduce.7
  238.0 1.3 compare_and_fusion
  239.3 1.8 fusion.8
  241.2 1.0 fusion.10
  242.2 1.1 fusion.49
  243.4 6.4 %copy.21 = bf16[16,256,512]{2,1,0:T(8,128)(2,1)} copy(bf16[16,256,512]{1,2,0:T(8,128)(2,1)} %bitcast.208) | data formatting | bytes 8388608 | tf_op jit(solution)/shard_map/tw,cwd->tcd/dot_general | solution.py:233
  249.8 3.7 %fusion.7 = bf16[1,128,4096]{2,1,0:T(8,128)(2,1)S(1)} fusion(bf16[128,512]{0,1:T(8,128)(2,1)S(1)} %bitcast.215, bf16[4096,512]{1,0:T(8,128)(2,1)} %bitcast.204, f32[1,1,128,4096]{3,2,1,0:T(8,128)S(1)} %copy-done.1), kind=kOutput, calls=%fused_computation.10 | convolution fusion | flops 537919488 | bytes 7471104 | tf_op jit(solution)/shard_map/tw,cwd->tcd/dot_general | solution.py:233
  253.5 0.9 slice_convert_fusion
  254.4 6.4 %copy.26 = bf16[16,256,512]{2,1,0:T(8,128)(2,1)} copy(bf16[16,256,512]{1,2,0:T(8,128)(2,1)} %bitcast.207) | data formatting | bytes 8388608 | tf_op jit(solution)/shard_map/tw,cwd->tcd/dot_general | solution.py:233
  261.4 4.8 %fusion.34 = bf16[128,768]{1,0:T(8,128)(2,1)S(1)} fusion(bf16[16,272,768]{2,1,0:T(8,128)(2,1)} %get-tuple-element.11, f32[128,16,256]{2,1,0:T(8,128)S(1)} %bitcast.209, f32[16,256]{1,0:T(8,128)S(1)} %bitcast.219, f32[128]{0:T(128)S(1)} %add_rsqrt_fusion), kind=kOutput, calls=%fused_computation.39 | convolution fusion | flops 806977536 | bytes 8602112 | tf_op jit(solution)/shard_map/tcd,cdw->tw/dot_general | solution.py:222
  266.3 0.6 slice.72.refs_0_
  266.9 18.7 %shard_map.75 = bf16[16,128,256]{2,1,0:T(8,128)(2,1)} custom-call(bf16[128,256]{1,0:T(8,128)(2,1)} %slice.72.refs_0_), custom_call_target="tpu_custom_call" | custom-call | tf_op jit(solution)/shard_map/pallas_call | solution.py:137
  285.7 1.8 fusion.9
  287.5 1.0 fusion.12
  288.6 1.1 fusion.55
  289.7 1.1 copy-done.2
  290.7 1.5 fusion.6
  292.3 2.6 collective-permute-done.1
  295.0 1.5 bitcast_convert_fusion
  (29 shorter events, 1.8 us)
Async XLA Ops:
  0.0 198.9 %copy-start.1 = (f32[1,1,128,4096]{3,2,1,0:T(8,128)S(1)}, f32[1,1,128,4096]{3,2,1,0:T(8,128)}, u32[]{:S(2)}) copy-start(f32[1,1,128,4096]{3,2,1,0:T(8,128)} %param.7) | copy-start | bytes 6291460
  199.8 35.5 %copy-start = (s32[1,2048]{1,0:T(1,128)S(1)}, s32[1,2048]{1,0:T(1,128)}, u32[]{:S(2)}) copy-start(s32[1,2048]{1,0:T(1,128)} %param.12) | copy-start | bytes 24580
  239.3 2.9 copy-start.3
  253.5 7.4 %collective-permute-start = (bf16[1,128,4096]{2,1,0:T(8,128)(2,1)S(1)}, bf16[1,128,4096]{2,1,0:T(8,128)(2,1)S(1)}, u32[]{:S(2)}, u32[]{:S(2)}) collective-permute-start(bf16[1,128,4096]{2,1,0:T(8,128)(2,1)S(1)} %fusion.7), channel_id=1, source_target_pairs={{0,1},{1,0},{2,3},{3,2},{4,5},{5,4},{6,7},{7,6},{8,9},{9,8},{10,11... | collective-permute-start | bytes 3145736 | tf_op jit(solution)/shard_map/ppermute | solution.py:17
  285.6 2.9 copy-start.4
  288.6 2.2 copy-start.2
  292.3 2.7 collective-permute-start.1

commit v2 on v1

v2 whole, which is shorter than its diff:
```python
import functools
import itertools
import math

import jax
import jax.numpy as jnp
from jax import lax
from jax.experimental import pallas as pl
from jax.experimental.pallas import tpu as pltpu
from jax.sharding import PartitionSpec as P

TICKS = 2


def passed_along(array, axis, by):
    length = lax.axis_size(axis)
    return lax.ppermute(array, axis, [(i, (i + by) % length) for i in range(length)])


def grid_of(count):
    known = {16: (4, 2, 2), 32: (4, 8)}
    return known.get(count, (count,))


def orders_of(sizes):
    dims = tuple(range(len(sizes)))
    if len(dims) == 1:
        return (dims, dims)
    return (dims, dims[:-2] + (dims[-1], dims[-2]))


def layers_kernel(sizes, cuts, *refs):
    weights = 2 * TICKS
    count = len(cuts)
    stream, bias = refs[0], refs[1]
    out = refs[2 + weights]
    scratch = refs[3 + weights :]
    blocks = refs[2 : 2 + weights] + scratch[:TICKS]
    wholes = scratch[TICKS : TICKS + count]
    queries, attended, leaving, arriving = scratch[TICKS + count : TICKS + count + 4]
    send_sems, recv_sems, own_sems, pipe_sems = scratch[TICKS + count + 4 :]
    rank = len(sizes)
    strides = [math.prod(sizes[d + 1 :]) for d in range(rank)]
    ctx_count = math.prod(sizes)
    me = lax.axis_index("ctx")
    coords = [(me // strides[d]) % sizes[d] for d in range(rank)]
    pipe_count = lax.axis_size("pipe")
    section = lax.axis_index("pipe")

    def place(delta):
        return sum(((coords[d] + delta[d]) % sizes[d]) * strides[d] for d in range(rank))

    def along(dim, by):
        return tuple(by if d == dim else 0 for d in range(rank))

    def flat(delta):
        return sum(delta[d] * strides[d] for d in range(rank))

    barrier = pltpu.get_barrier_semaphore()
    greeted = 0
    for dim in range(rank):
        for by in range(1, sizes[dim]):
            pl.semaphore_signal(
                barrier,
                inc=1,
                device_id={"ctx": place(along(dim, by))},
                device_id_type=pl.DeviceIdType.MESH,
            )
            greeted += 1
    for by in sorted({1, pipe_count - 1}):
        pl.semaphore_signal(
            barrier,
            inc=1,
            device_id={"pipe": (section + by) % pipe_count},
            device_id_type=pl.DeviceIdType.MESH,
        )
        greeted += 1
    pl.semaphore_wait(barrier, greeted)

    orders = orders_of(sizes)
    started = []
    used = {}

    def copy_of(which, part, delta, dim, by, send):
        rows = pl.ds(*cuts[which][part])
        landing = wholes[which].at[place(delta), rows]
        origin = landing if any(delta) else blocks[which].at[rows]
        seen = tuple((sizes[d] - by) % sizes[d] if d == dim else delta[d] for d in range(rank))
        return pltpu.make_async_remote_copy(
            src_ref=origin,
            dst_ref=landing,
            send_sem=send_sems.at[which, part, send],
            recv_sem=recv_sems.at[which, part, flat(seen)],
            device_id={"ctx": place(along(dim, by))},
            device_id_type=pl.DeviceIdType.MESH,
        )

    def pass_on(which, part, delta, phases):
        for phase in phases:
            dim = orders[part][phase]
            for by in range(1, sizes[dim]):
                send = used.get((which, part), 0)
                used[which, part] = send + 1
                copy = copy_of(which, part, delta, dim, by, send)
                copy.start()
                started.append(copy)

    def take(which, phase):
        for part, order in enumerate(orders):
            ranges = [range(1)] * rank
            for before in order[:phase]:
                ranges[before] = range(sizes[before])
            ranges[order[phase]] = range(1, sizes[order[phase]])
            for delta in itertools.product(*ranges):
                landing = wholes[which].at[place(delta), pl.ds(*cuts[which][part])]
                pltpu.make_async_remote_copy(
                    src_ref=landing,
                    dst_ref=landing,
                    send_sem=send_sems.at[which, part, 0],
                    recv_sem=recv_sems.at[which, part, flat(delta)],
                    device_id={"ctx": place(along(order[phase], 1))},
                    device_id_type=pl.DeviceIdType.MESH,
                ).wait_recv()
                pass_on(which, part, delta, range(phase + 1, rank))

    def own_copy(which):
        return pltpu.make_async_copy(blocks[which], wholes[which].at[me], own_sems.at[which])

    def begin(which):
        own_copy(which).start()
        for part in range(len(orders)):
            pass_on(which, part, (0,) * rank, range(rank))

    tok_rows, model_width = stream.shape
    in_rows = model_width // ctx_count
    query_width = attended.shape[1]
    head_dim = queries.shape[-1]
    head_count = query_width // head_dim
    scale = 1.0 / math.sqrt(head_dim)

    def columns(index):
        return pl.ds(pl.multiple_of(index * in_rows, in_rows), in_rows)

    def project(tick, source):
        own_copy(2 * tick).wait()
        whole = wholes[2 * tick]

        def square(index, total):
            value = source[:, columns(index)].astype(jnp.float32)
            return total + jnp.sum(value * value, axis=1, keepdims=True)

        squares = lax.fori_loop(0, ctx_count, square, jnp.zeros((tok_rows, 1), jnp.float32))
        factor = lax.rsqrt(squares / model_width + 1e-05)

        def piece(index, total):
            value = source[:, columns(index)].astype(jnp.float32)
            gain = whole[index, in_rows : in_rows + 16, :in_rows].astype(jnp.float32)[:1]
            hidden = (value * factor * gain).astype(jnp.bfloat16)
            return total + jnp.dot(
                hidden, whole[index, :in_rows, :], preferred_element_type=jnp.float32
            )

        width = whole.shape[-1]
        sums = lax.fori_loop(0, ctx_count, piece, jnp.zeros((tok_rows, width), jnp.float32))
        low = sums.astype(jnp.bfloat16)
        for head in range(head_count):
            queries[head] = low[:, head * head_dim : (head + 1) * head_dim]
        blocks[weights + tick][...] = low[:, query_width:]

    def attend(tick):
        own_copy(weights + tick).wait()
        whole = wholes[weights + tick]
        keys = whole[:, :, :head_dim].reshape(ctx_count * tok_rows, head_dim)
        values = whole[:, :, head_dim:].reshape(ctx_count * tok_rows, head_dim)
        for head in range(head_count):
            scores = lax.dot_general(
                queries[head], keys, (((1,), (1,)), ((), ())), preferred_element_type=jnp.float32
            )
            scores = scores * scale + bias[...]
            probs = jnp.exp(scores - jnp.max(scores, axis=1, keepdims=True))
            totals = jnp.sum(probs, axis=1, keepdims=True)
            summed = jnp.dot(
                probs.astype(jnp.bfloat16), values, preferred_element_type=jnp.float32
            )
            attended[:, head * head_dim : (head + 1) * head_dim] = (summed / totals).astype(
                jnp.bfloat16
            )

    def mix(tick, source, target):
        own_copy(2 * tick + 1).wait()
        whole = wholes[2 * tick + 1]

        @pl.loop(0, ctx_count)
        def _(index):
            mixed = jnp.dot(attended[...], whole[index], preferred_element_type=jnp.float32)
            value = source[:, columns(index)].astype(jnp.float32) + mixed
            target[:, columns(index)] = value.astype(jnp.bfloat16)

    last = rank - 1
    begin(0)
    begin(1)
    take(0, 0)
    begin(2)
    for phase in range(1, rank):
        take(0, phase)
        take(1, phase - 1)
    project(0, stream)
    begin(4)
    begin(3)
    for phase in range(rank):
        take(4, phase)
        if phase < last:
            take(2, phase)
    attend(0)
    for phase in range(last):
        take(3, phase)
    take(1, last)
    mix(0, stream, leaving)
    onward = pltpu.make_async_remote_copy(
        src_ref=leaving,
        dst_ref=arriving,
        send_sem=pipe_sems.at[0],
        recv_sem=pipe_sems.at[1],
        device_id={"pipe": (section + 1) % pipe_count},
        device_id_type=pl.DeviceIdType.MESH,
    )
    onward.start()
    take(2, last)
    onward.wait()
    project(1, arriving)
    begin(5)
    for phase in range(rank):
        take(5, phase)
    attend(1)
    take(3, last)
    mix(1, arriving, out)
    for copy in started:
        copy.wait_send()


def run_layers(stream, bias, blocks, ctx_count, head_dim):
    tok_rows = stream.shape[0]
    query_width = blocks[1].shape[0]
    kv_width = blocks[0].shape[1] - query_width
    shapes = [block.shape for block in blocks] + [(tok_rows, kv_width)] * TICKS
    cuts = []
    for rows, _ in shapes:
        first = rows // 32 * 16
        cuts.append(((0, first), (first, rows - first)))
    count = len(shapes)
    parts = len(cuts[0])
    low = jnp.bfloat16
    vmem = pl.BlockSpec(memory_space=pltpu.VMEM)
    return pl.pallas_call(
        functools.partial(layers_kernel, grid_of(ctx_count), tuple(cuts)),
        out_shape=jax.ShapeDtypeStruct(stream.shape, low),
        in_specs=[vmem, vmem] + [pl.BlockSpec(memory_space=pl.ANY)] * len(blocks),
        out_specs=vmem,
        scratch_shapes=[pltpu.VMEM((tok_rows, kv_width), low)] * TICKS
        + [pltpu.VMEM((ctx_count, *shape), low) for shape in shapes]
        + [
            pltpu.VMEM((query_width // head_dim, tok_rows, head_dim), low),
            pltpu.VMEM((tok_rows, query_width), low),
            pltpu.VMEM(stream.shape, low),
            pltpu.VMEM(stream.shape, low),
            pltpu.SemaphoreType.DMA((count, parts, ctx_count)),
            pltpu.SemaphoreType.DMA((count, parts, ctx_count)),
            pltpu.SemaphoreType.DMA((count,)),
            pltpu.SemaphoreType.DMA((2,)),
        ],
        compiler_params=pltpu.CompilerParams(
            collective_id=0, has_side_effects=True, vmem_limit_bytes=56 * 1024 * 1024
        ),
    )(stream, bias, *blocks)


def row_positions(rows, tok_rows, ctx_count):
    half = tok_rows // 2
    block = rows // tok_rows
    offset = rows % tok_rows
    return jnp.where(
        offset < half, block * half + offset, (2 * ctx_count - 1 - block) * half + offset - half
    )


def pick(stacked, layer):
    return lax.dynamic_index_in_dim(stacked[0], layer, 0, keepdims=False)


def body(activations, norm_gain, w_query, w_keyval, w_out, segment_ids, layer_order):
    ctx_count = lax.axis_size("ctx")
    ctx_index = lax.axis_index("ctx")
    state = activations[0]
    seqs_here, tok_rows, model_width = state.shape
    query_width = w_query.shape[-1]
    kv_width = w_keyval.shape[-1]
    head_dim = kv_width // 2
    in_rows = w_query.shape[2]
    wide = query_width + kv_width
    in_parts, out_parts = [], []
    for tick in range(TICKS):
        layer = layer_order[tick, 0]
        gain_rows = jnp.pad(pick(norm_gain, layer)[None, :], ((0, 15), (0, wide - in_rows)))
        both = jnp.concatenate([pick(w_query, layer), pick(w_keyval, layer)], axis=1)
        in_parts.append(jnp.concatenate([both, gain_rows], axis=0))
        out_parts.append(pick(w_out, layer))
    query_pos = row_positions(
        ctx_index * tok_rows + lax.iota(jnp.int32, tok_rows), tok_rows, ctx_count
    )
    query_seg = jnp.take(segment_ids, query_pos, axis=1)
    halves = segment_ids.reshape(seqs_here, 2, ctx_count, tok_rows // 2)
    by_row = jnp.stack([halves[:, 0], halves[:, 1, ::-1]], axis=2)
    key_seg = by_row.reshape(seqs_here, ctx_count * tok_rows)
    key_pos = row_positions(lax.iota(jnp.int32, ctx_count * tok_rows), tok_rows, ctx_count)
    allowed = (key_pos[None, None, :] <= query_pos[None, :, None]) & (
        key_seg[:, None, :] == query_seg[:, :, None]
    )
    bias = jnp.where(allowed[0], 0.0, -1e30)
    blocks = [part for pair in zip(in_parts, out_parts) for part in pair]
    state = run_layers(state[0], bias, blocks, ctx_count, head_dim)
    state = passed_along(state, "pipe", 1).astype(jnp.float32)[None]
    return state[None]


def solution(mesh):
    in_specs = (
        P("pipe", None, "ctx", None),
        P("pipe", None, "ctx"),
        P("pipe", None, "ctx", None),
        P("pipe", None, "ctx", None),
        P("pipe", None, None, "ctx"),
        P(),
        P(None, "pipe"),
    )
    out_specs = P("pipe", None, "ctx", None)
    return jax.shard_map(body, mesh=mesh, in_specs=in_specs, out_specs=out_specs, check_vma=False)
```

time: 297 us -> 257 us (0.87)
  matrix products: 20.8 us -> 0 us
  local copies, waits for them, and re-layouts: 24.3 us -> 8.39 us
  other arithmetic: 8.84 us -> 5.19 us
    dot_general x8 -> x0, matrix products: 20.8 us -> none  [the longest x2 9.65 us: body(): jnp.einsum('tcd,cdw->tw', hidden.reshape(seqs_here * tok_rows, ctx_count,...]
    dot_general x2 -> x0, local copies, waits for them, and re-layouts: 12.8 us -> none  [body(): jnp.einsum('tw,cwd->tcd', attended, out_all, preferred_element_type=jnp.f...]
    pallas_call x3 -> x1, Pallas kernels: 236 us -> 236 us  [run_layers(): pl.pallas_call(functools.partial(layers_kernel, grid_of(ctx_count), tuple...]
  transfers between devices with their start and end apart: 2 -> 1, of which waited for: 1 -> 1; matrix products, arithmetic and copies ran while one was open for 2% -> 0% of each run, Pallas kernels for 0% -> 0%
where the time goes in v2:
time: 257 us; the launch traced here: 256 us
  Pallas kernels  236 us (92%)
  local copies, waits for them, and re-layouts  8.39 us (3%)
  other arithmetic  5.19 us (2%)
  between operations  3.82 us (1%)
  waiting for transfers between devices  2.86 us (1%)
    pallas_call x1, Pallas kernels, run_layers(): pl.pallas_call(functools.partial(layers_kernel, grid_of(ctx_count), tuple...  236 us
  transfers between devices with their start and end apart: 1, of which 1 were waited for; matrix products, arithmetic and copies ran while one was open for 0% of the time, Pallas kernels for 0%

profile of v2, /device:TPU:0, one launch (start us, length us, event | category | flops | bytes accessed | tf_op | source)
XLA Modules:
  0.0 256.4 jit_solution(10577562339851064461)
XLA Ops:
  0.0 1.4 fusion.23
  4.0 1.6 gather_fusion
  5.6 0.5 broadcast.494
  6.1 1.4 reduce.3
  7.5 0.1 reshape.256
  7.6 0.1 eq.22
  8.9 0.8 fusion.20
  9.7 1.0 dynamic-slice_bitcast_fusion.4
  10.7 1.9 dynamic-slice_bitcast_fusion
  12.6 1.1 dynamic-slice_bitcast_fusion.1
  13.6 1.2 and_select_fusion.refs_1_
  14.8 1.0 fusion.2
  15.9 236.1 %shard_map.73 = bf16[128,4096]{1,0:T(8,128)(2,1)} custom-call(f32[128,4096]{1,0:T(8,128)} %bitcast.30, f32[128,2048]{1,0:T(8,128)} %and_select_fusion.refs_1_, bf16[272,768]{1,0:T(8,128)(2,1)} %get-tuple-element.19.refs_2_, bf16[512,256]{1,0:T(8,128)(2,1)} %get-tuple-element.6.refs_3_, bf16[272,768]{1,0:T(8,128)(2,1)} %get-tuple-element.20.refs_4_, ...), custom_call_target="tpu_custom_call" | custom-call | tf_op jit(solution)/shard_map/pallas_call | solution.py:254
  251.9 0.1 collective-permute-start
  252.0 2.9 %collective-permute-done = bf16[128,4096]{1,0:T(8,128)(2,1)S(1)} collective-permute-done((bf16[128,4096]{1,0:T(8,128)(2,1)}, bf16[128,4096]{1,0:T(8,128)(2,1)S(1)}, u32[]{:S(2)}, u32[]{:S(2)}) %collective-permute-start) | collective-permute-done | bytes 1048608 | tf_op jit(solution)/shard_map/ppermute | solution.py:17
  254.9 1.5 bitcast_convert_fusion
  (7 shorter events, 0.1 us)
Async XLA Ops:
  251.9 2.9 %collective-permute-start = (bf16[128,4096]{1,0:T(8,128)(2,1)}, bf16[128,4096]{1,0:T(8,128)(2,1)S(1)}, u32[]{:S(2)}, u32[]{:S(2)}) collective-permute-start(bf16[128,4096]{1,0:T(8,128)(2,1)} %shard_map.73), channel_id=1, source_target_pairs={{0,1},{1,0},{2,3},{3,2},{4,5},{5,4},{6,7},{7,6},{8,9},{9,8},{10,11... | collective-permute-start | bytes 3145736 | tf_op jit(solution)/shard_map/ppermute | solution.py:17

commit v3 on v2

--- a/solution.py
+++ b/solution.py
@@ -154,7 +154,8 @@
 
         def piece(index, total):
             value = source[:, columns(index)].astype(jnp.float32)
-            gain = whole[index, in_rows : in_rows + 16, :in_rows].astype(jnp.float32)[:1]
+            gain = wholes[0][index, in_rows : in_rows + 16, :in_rows].astype(jnp.float32)
+            gain = gain[tick : tick + 1]
             hidden = (value * factor * gain).astype(jnp.bfloat16)
             return total + jnp.dot(
                 hidden, whole[index, :in_rows, :], preferred_element_type=jnp.float32
@@ -300,17 +301,20 @@
     in_parts, out_parts = [], []
     for tick in range(TICKS):
         layer = layer_order[tick, 0]
-        gain_rows = jnp.pad(pick(norm_gain, layer)[None, :], ((0, 15), (0, wide - in_rows)))
         both = jnp.concatenate([pick(w_query, layer), pick(w_keyval, layer)], axis=1)
-        in_parts.append(jnp.concatenate([both, gain_rows], axis=0))
+        if tick == 0:
+            gains = jnp.stack([pick(norm_gain, layer_order[t, 0]) for t in range(TICKS)])
+            gains = jnp.pad(gains, ((0, 16 - TICKS), (0, wide - in_rows)))
+            both = jnp.concatenate([both, gains], axis=0)
+        in_parts.append(both)
         out_parts.append(pick(w_out, layer))
     query_pos = row_positions(
         ctx_index * tok_rows + lax.iota(jnp.int32, tok_rows), tok_rows, ctx_count
     )
-    query_seg = jnp.take(segment_ids, query_pos, axis=1)
     halves = segment_ids.reshape(seqs_here, 2, ctx_count, tok_rows // 2)
     by_row = jnp.stack([halves[:, 0], halves[:, 1, ::-1]], axis=2)
     key_seg = by_row.reshape(seqs_here, ctx_count * tok_rows)
+    query_seg = lax.dynamic_slice_in_dim(key_seg, ctx_index * tok_rows, tok_rows, axis=1)
     key_pos = row_positions(lax.iota(jnp.int32, ctx_count * tok_rows), tok_rows, ctx_count)
     allowed = (key_pos[None, None, :] <= query_pos[None, :, None]) & (
         key_seg[:, None, :] == query_seg[:, :, None]

time: 257 us -> 253 us (0.984)
  no operation moved by 1% of the time
where the time goes in v3:
time: 253 us
  Pallas kernels  234 us (92%)
  local copies, waits for them, and re-layouts  6.79 us (3%)
  other arithmetic  5.71 us (2%)
  between operations  3.6 us (1%)
  waiting for transfers between devices  2.86 us (1%)
    pallas_call x1, Pallas kernels, run_layers(): pl.pallas_call(functools.partial(layers_kernel, grid_of(ctx_count), tuple...  234 us
  transfers between devices with their start and end apart: 1, of which 1 were waited for; matrix products, arithmetic and copies ran while one was open for 0% of the time, Pallas kernels for 0%

profile of v3, /device:TPU:0, one launch (start us, length us, event | category | flops | bytes accessed | tf_op | source)
XLA Modules:
  0.0 252.9 jit_solution(10961052361624748893)
XLA Ops:
  0.0 1.3 fusion.25
  3.7 0.5 broadcast.211
  4.2 1.4 reduce.3
  5.6 0.1 reshape.133
  5.7 0.1 reshape.134
  5.8 0.1 eq.24
  7.0 0.8 fusion.21
  7.8 1.0 dynamic-slice_bitcast_fusion.4
  8.8 1.9 dynamic-slice_bitcast_fusion
  10.7 1.1 dynamic-slice_bitcast_fusion.1
  11.8 0.8 pad_maximum_fusion.1.refs_4_
  12.6 0.8 pad_maximum_fusion.refs_2_
  13.4 1.2 and_select_fusion.refs_1_
  14.6 233.9 %shard_map.73 = bf16[128,4096]{1,0:T(8,128)(2,1)} custom-call(f32[128,4096]{1,0:T(8,128)} %bitcast.28, f32[128,2048]{1,0:T(8,128)} %and_select_fusion.refs_1_, bf16[272,768]{1,0:T(8,128)(2,1)} %pad_maximum_fusion.refs_2_, bf16[512,256]{1,0:T(8,128)(2,1)} %get-tuple-element.6.refs_3_, bf16[256,768]{1,0:T(8,128)(2,1)} %pad_maximum_fusion.1.refs_4_, ...), custom_call_target="tpu_custom_call" | custom-call | tf_op jit(solution)/shard_map/pallas_call | solution.py:255
  248.4 0.1 collective-permute-start
  248.5 2.9 %collective-permute-done = bf16[128,4096]{1,0:T(8,128)(2,1)S(1)} collective-permute-done((bf16[128,4096]{1,0:T(8,128)(2,1)}, bf16[128,4096]{1,0:T(8,128)(2,1)S(1)}, u32[]{:S(2)}, u32[]{:S(2)}) %collective-permute-start) | collective-permute-done | bytes 1048608 | tf_op jit(solution)/shard_map/ppermute | solution.py:17
  251.4 1.5 bitcast_convert_fusion
  (7 shorter events, 0.1 us)
Async XLA Ops:
  248.4 2.9 %collective-permute-start = (bf16[128,4096]{1,0:T(8,128)(2,1)}, bf16[128,4096]{1,0:T(8,128)(2,1)S(1)}, u32[]{:S(2)}, u32[]{:S(2)}) collective-permute-start(bf16[128,4096]{1,0:T(8,128)(2,1)} %shard_map.73), channel_id=1, source_target_pairs={{0,1},{1,0},{2,3},{3,2},{4,5},{5,4},{6,7},{7,6},{8,9},{9,8},{10,11... | collective-permute-start | bytes 3145736 | tf_op jit(solution)/shard_map/ppermute | solution.py:17
